TPU v7x, 32 devices: a whole 2x2x4 slice. The times are simulated.
32 devices in a mesh: seq: 16 (over z, y, x), tp: 2 (over core).
Axes of the slice: x: 2, y: 2, z: 4, core: 2. Of those that a mesh axis runs over, the one named last changes fastest.
Arguments:
- conv_in: bfloat16 [4096, 16384], P('seq', 'tp'), may hold values from -6 to 6
- gate_in: bfloat16 [4096, 16384], P('seq', 'tp'), may hold values from -6 to 6
- q_proj: bfloat16 [4096, 8192], P('seq', 'tp'), may hold values from -6 to 6
- k_proj: bfloat16 [4096, 1024], P('seq', 'tp'), may hold values from -6 to 6
- v_proj: bfloat16 [4096, 1024], P('seq', 'tp'), may hold values from -6 to 6
- conv_weight: float32 [4, 16384], P(None, 'tp'), may hold values from -3 to 3
- conv_bias: float32 [16384], P('tp'), may hold values from -0.5 to 0.5
- proj_dt_weight: bfloat16 [16384, 512], P('tp'), may hold values from -0.046875 to 0.046875
- proj_bc_weight: bfloat16 [32, 16384], P(None, 'tp'), may hold values from -0.046875 to 0.046875
- dt_gain: float32 [512], replicated, may hold values from 0.1 to 1.9
- dt_weight: bfloat16 [512, 16384], P(None, 'tp'), may hold values from -0.25 to 0.25
- dt_bias: float32 [16384], P('tp'), may hold values from -5 to -2
- decay_rate: float32 [16, 16384], P(None, 'tp'), may hold values from 1e-05 to 2
- skip_weight: float32 [16384], P('tp'), may hold values from 0.5 to 1.5
Outputs:
- mamba_out: bfloat16 [4096, 16384], P('seq', 'tp')
- attn_out: bfloat16 [4096, 8192], P('seq', 'tp')
All inputs are finite; a program needn't handle non-finite values.
Results may differ from a plain program's by a relative error of at most 0.0051.
Values may be sent and summed in bfloat16 or wider, within the bound.
A program may use at most 192 MiB of HBM per device.

v0:
```python
import functools
import math

import jax
import jax.numpy as jnp
from jax import lax
from jax.experimental import pallas as pl
from jax.experimental.pallas import tpu as pltpu
from jax.sharding import PartitionSpec as P

KCONV = 4
HD = 128
WINDOW = 2048
LANES = 128
SUBLANES = 8
GROUP = LANES * SUBLANES
TAIL = 16
LOG2E = math.log2(math.e)
FAR = -1e30
epsilon = 1e-06


def shifted(value, axis, steps):
    count = lax.axis_size(axis)
    return lax.ppermute(value, axis, [(source, source + steps) for source in range(count - steps)])


def params(mib=56):
    return pltpu.CompilerParams(vmem_limit_bytes=mib * 1024 * 1024)


def project_kernel(rank, tail_ref, x_ref, taps_ref, bias_ref, wdt_ref, wbc_ref, act_ref, sums_ref, wide):
    tokens = x_ref.shape[0]
    wide[:TAIL] = tail_ref[...].astype(jnp.float32)
    wide[TAIL:] = x_ref[...].astype(jnp.float32)
    total = bias_ref[...] + taps_ref[0:1] * wide[pl.ds(TAIL - 3, tokens)]
    for j in range(1, KCONV):
        total = total + taps_ref[j : j + 1] * wide[pl.ds(TAIL - 3 + j, tokens)]
    act = (total / (1.0 + jnp.exp(-total))).astype(jnp.bfloat16)
    act_ref[...] = act
    low = jnp.dot(act, wdt_ref[...], preferred_element_type=jnp.float32)
    state = lax.dot_general(
        act, wbc_ref[...], (((1,), (1,)), ((), ())), preferred_element_type=jnp.float32
    )
    states = state.shape[1]

    @pl.when(pl.program_id(0) == 0)
    def _():
        sums_ref[...] = jnp.zeros_like(sums_ref)

    sums_ref[:, :rank] += low
    sums_ref[:, rank : rank + states] += state


def project(tail, conv_in, taps, bias, wdt, wbc):
    tokens, channels = conv_in.shape
    rank = wdt.shape[1]
    states = wbc.shape[0]
    blocks = channels // GROUP
    return pl.pallas_call(
        functools.partial(project_kernel, rank),
        grid=(blocks,),
        in_specs=[
            pl.BlockSpec((TAIL, GROUP), lambda i: (0, i)),
            pl.BlockSpec((tokens, GROUP), lambda i: (0, i)),
            pl.BlockSpec((KCONV, GROUP), lambda i: (0, i)),
            pl.BlockSpec((1, GROUP), lambda i: (0, i)),
            pl.BlockSpec((GROUP, rank), lambda i: (i, 0)),
            pl.BlockSpec((states, GROUP), lambda i: (0, i)),
        ],
        out_specs=[
            pl.BlockSpec((tokens, GROUP), lambda i: (0, i)),
            pl.BlockSpec((tokens, rank + LANES), lambda i: (0, 0)),
        ],
        out_shape=[
            jax.ShapeDtypeStruct((tokens, channels), jnp.bfloat16),
            jax.ShapeDtypeStruct((tokens, rank + LANES), jnp.float32),
        ],
        scratch_shapes=[pltpu.VMEM((TAIL + tokens, GROUP), jnp.float32)],
        compiler_params=params(),
        cost_estimate=pl.CostEstimate(
            flops=2 * tokens * channels * (rank + states),
            bytes_accessed=4 * tokens * channels + 2 * channels * rank,
            transcendentals=tokens * channels,
        ),
        name="conv_and_projections",
    )(tail, conv_in, taps, bias, wdt, wbc)


def scan_kernel(rank, state_count, bc_ref, low_ref, gain_ref, wdt_ref, bias_ref, act_ref, rate_ref,
                y_ref, cum_ref, final_ref, normed, steps, drives):
    tokens = act_ref.shape[0]

    @pl.when(pl.program_id(0) == 0)
    def _():
        low = low_ref[:, :rank]
        mean_square = jnp.mean(low * low, axis=-1, keepdims=True)
        normed[...] = (low * lax.rsqrt(mean_square + epsilon) * gain_ref[...]).astype(jnp.bfloat16)

    for j in range(SUBLANES):
        cols = slice(j * LANES, (j + 1) * LANES)
        raw = (
            jnp.dot(normed[...], wdt_ref[:, cols], preferred_element_type=jnp.float32)
            + bias_ref[:, cols]
        )
        step = jnp.maximum(raw, 0.0) + jnp.log1p(jnp.exp(-jnp.abs(raw)))
        steps[pl.ds(j, tokens, stride=SUBLANES), :] = step
        drives[pl.ds(j, tokens, stride=SUBLANES), :] = step * act_ref[:, cols].astype(jnp.float32)

    def advance(t, carry):
        through, hidden = carry
        rows = pl.ds(pl.multiple_of(t * SUBLANES, SUBLANES), SUBLANES)
        step, drive = steps[rows, :], drives[rows, :]
        base = t * (2 * state_count)
        out = None
        new = []
        for n in range(state_count):
            h = jnp.exp2(rate_ref[0, n] * step) * hidden[n] + bc_ref[base + n] * drive
            term = bc_ref[base + state_count + n] * h
            out = term if out is None else out + term
            new.append(h)
        through = through + step
        y_ref[0, rows, :] = out
        cum_ref[0, rows, :] = through
        return through, tuple(new)

    zero = jnp.zeros((SUBLANES, LANES), jnp.float32)
    _, hidden = lax.fori_loop(0, tokens, advance, (zero, (zero,) * state_count), unroll=4)
    for n in range(state_count):
        final_ref[0, n] = hidden[n]


def local_scan(bc, low, gain, wdt, bias, act, rates):
    tokens, channels = act.shape
    rank = gain.shape[1]
    blocks, state_count = rates.shape[:2]
    rows = tokens * SUBLANES
    return pl.pallas_call(
        functools.partial(scan_kernel, rank, state_count),
        grid=(blocks,),
        in_specs=[
            pl.BlockSpec(memory_space=pltpu.SMEM),
            pl.BlockSpec(low.shape, lambda i: (0, 0)),
            pl.BlockSpec((1, rank), lambda i: (0, 0)),
            pl.BlockSpec((rank, GROUP), lambda i: (0, i)),
            pl.BlockSpec((1, GROUP), lambda i: (0, i)),
            pl.BlockSpec((tokens, GROUP), lambda i: (0, i)),
            pl.BlockSpec((1, state_count, SUBLANES, LANES), lambda i: (i, 0, 0, 0)),
        ],
        out_specs=[
            pl.BlockSpec((1, rows, LANES), lambda i: (i, 0, 0)),
            pl.BlockSpec((1, rows, LANES), lambda i: (i, 0, 0)),
            pl.BlockSpec((1, state_count, SUBLANES, LANES), lambda i: (i, 0, 0, 0)),
        ],
        out_shape=[
            jax.ShapeDtypeStruct((blocks, rows, LANES), jnp.float32),
            jax.ShapeDtypeStruct((blocks, rows, LANES), jnp.float32),
            jax.ShapeDtypeStruct((blocks, state_count, SUBLANES, LANES), jnp.float32),
        ],
        scratch_shapes=[
            pltpu.VMEM((tokens, rank), jnp.bfloat16),
            pltpu.VMEM((rows, LANES), jnp.float32),
            pltpu.VMEM((rows, LANES), jnp.float32),
        ],
        compiler_params=params(),
        cost_estimate=pl.CostEstimate(
            flops=2 * tokens * channels * rank + 8 * tokens * channels * state_count,
            bytes_accessed=12 * tokens * channels + 2 * channels * rank,
            transcendentals=tokens * channels * state_count,
        ),
        name="local_scan",
    )(bc, low, gain, wdt, bias, act, rates)


def finish_kernel(state_count, bc_ref, y_ref, cum_ref, rate_ref, enter_ref, act_ref, gate_ref, skip_ref,
                  out_ref, mixed):
    tokens = act_ref.shape[0]

    def adjust(t, carry):
        rows = pl.ds(pl.multiple_of(t * SUBLANES, SUBLANES), SUBLANES)
        through = cum_ref[0, rows, :]
        base = t * (2 * state_count) + state_count
        total = y_ref[0, rows, :]
        for n in range(state_count):
            total = total + bc_ref[base + n] * (jnp.exp2(rate_ref[0, n] * through) * enter_ref[0, n])
        mixed[rows, :] = total
        return carry

    lax.fori_loop(0, tokens, adjust, 0, unroll=4)
    for j in range(SUBLANES):
        cols = slice(j * LANES, (j + 1) * LANES)
        gate = gate_ref[:, cols].astype(jnp.float32)
        value = mixed[pl.ds(j, tokens, stride=SUBLANES), :]
        value = value + skip_ref[:, cols] * act_ref[:, cols].astype(jnp.float32)
        out_ref[:, cols] = (value * (gate / (1.0 + jnp.exp(-gate)))).astype(jnp.bfloat16)


def finish(bc, y, cum, rates, enter, act, gate, skip):
    tokens, channels = act.shape
    blocks, state_count = rates.shape[:2]
    rows = tokens * SUBLANES
    return pl.pallas_call(
        functools.partial(finish_kernel, state_count),
        grid=(blocks,),
        in_specs=[
            pl.BlockSpec(memory_space=pltpu.SMEM),
            pl.BlockSpec((1, rows, LANES), lambda i: (i, 0, 0)),
            pl.BlockSpec((1, rows, LANES), lambda i: (i, 0, 0)),
            pl.BlockSpec((1, state_count, SUBLANES, LANES), lambda i: (i, 0, 0, 0)),
            pl.BlockSpec((1, state_count, SUBLANES, LANES), lambda i: (i, 0, 0, 0)),
            pl.BlockSpec((tokens, GROUP), lambda i: (0, i)),
            pl.BlockSpec((tokens, GROUP), lambda i: (0, i)),
            pl.BlockSpec((1, GROUP), lambda i: (0, i)),
        ],
        out_specs=pl.BlockSpec((tokens, GROUP), lambda i: (0, i)),
        out_shape=jax.ShapeDtypeStruct((tokens, channels), jnp.bfloat16),
        scratch_shapes=[pltpu.VMEM((rows, LANES), jnp.float32)],
        compiler_params=params(),
        cost_estimate=pl.CostEstimate(
            flops=6 * tokens * channels * state_count,
            bytes_accessed=14 * tokens * channels,
            transcendentals=tokens * channels * state_count,
        ),
        name="carry_and_gate",
    )(bc, y, cum, rates, enter, act, gate, skip)


def attention_kernel(span, aliased, *refs):
    position, q_ref = refs[:2]
    key_refs = refs[2 : 3 + span]
    value_refs = refs[3 + span : 4 + 2 * span]
    out_ref, keys, values, scores = refs[4 + 2 * span + aliased :]
    tokens = q_ref.shape[0]

    @pl.when(pl.program_id(0) == 0)
    def _():
        first = lax.broadcasted_iota(jnp.int32, (tokens, HD), 1) == 0
        for d in range(span + 1):
            rows = slice(d * tokens, (d + 1) * tokens)
            absent = jnp.where(position[0] >= d, 0.0, FAR)
            keys[rows, :HD] = key_refs[d][...]
            keys[rows, HD:] = jnp.where(first, absent, 0.0).astype(jnp.bfloat16)
            values[rows, :HD] = value_refs[d][...]
            values[rows, HD:] = jnp.ones((tokens, HD), jnp.bfloat16)

    ones = (lax.broadcasted_iota(jnp.int32, (tokens, HD), 1) == 0).astype(jnp.bfloat16)
    query = jnp.concatenate([q_ref[...], ones], axis=1)
    near = lax.broadcasted_iota(jnp.int32, (tokens, tokens), 1) <= lax.broadcasted_iota(
        jnp.int32, (tokens, tokens), 0
    )

    def score(d):
        return lax.dot_general(
            query,
            keys[d * tokens : (d + 1) * tokens],
            (((1,), (1,)), ((), ())),
            preferred_element_type=jnp.float32,
        )

    block = jnp.where(near, score(0), score(span))
    scores[0] = block
    peak = block
    for d in range(1, span):
        block = score(d)
        scores[d] = block
        peak = jnp.maximum(peak, block)
    factor = LOG2E / math.sqrt(HD)
    peak = jnp.max(peak, axis=-1, keepdims=True) * factor
    weight = jnp.exp2(scores[0] * factor - peak).astype(jnp.bfloat16)
    zero = jnp.zeros_like(weight)
    total = jnp.dot(
        jnp.where(near, weight, zero), values[:tokens], preferred_element_type=jnp.float32
    ) + jnp.dot(
        jnp.where(near, zero, weight), values[span * tokens :], preferred_element_type=jnp.float32
    )
    for d in range(1, span):
        weight = jnp.exp2(scores[d] * factor - peak).astype(jnp.bfloat16)
        total = total + jnp.dot(
            weight, values[d * tokens : (d + 1) * tokens], preferred_element_type=jnp.float32
        )
    out_ref[...] = (total[:, :HD] / total[:, HD:]).astype(jnp.bfloat16)


def attention(head, position, queries, pairs, before):
    tokens, width = queries.shape
    span = len(pairs) - 1
    kv_here = pairs[0].shape[1] // (2 * HD)
    grouping = width // HD // kv_here
    aliased = 0 if before is None else 1
    specs = [
        pl.BlockSpec(memory_space=pltpu.SMEM),
        pl.BlockSpec((tokens, HD), lambda i: (0, head * grouping + i)),
    ]
    specs += [pl.BlockSpec((tokens, HD), lambda i: (0, head))] * (span + 1)
    specs += [pl.BlockSpec((tokens, HD), lambda i: (0, kv_here + head))] * (span + 1)
    operands = [position, queries, *pairs, *pairs]
    if aliased:
        specs.append(pl.BlockSpec(memory_space=pl.ANY))
        operands.append(before)
    keys = tokens * (span + 1)
    return pl.pallas_call(
        functools.partial(attention_kernel, span, aliased),
        grid=(grouping,),
        in_specs=specs,
        out_specs=pl.BlockSpec((tokens, HD), lambda i: (0, head * grouping + i)),
        out_shape=jax.ShapeDtypeStruct((tokens, width), jnp.bfloat16),
        scratch_shapes=[
            pltpu.VMEM((keys, 2 * HD), jnp.bfloat16),
            pltpu.VMEM((keys, 2 * HD), jnp.bfloat16),
            pltpu.VMEM((span, tokens, tokens), jnp.float32),
        ],
        input_output_aliases={len(operands) - 1: 0} if aliased else {},
        compiler_params=params(),
        cost_estimate=pl.CostEstimate(
            flops=8 * grouping * tokens * keys * HD,
            bytes_accessed=4 * tokens * grouping * HD + 4 * keys * HD,
            transcendentals=grouping * tokens * keys,
        ),
        name="window_attention",
    )(*operands)


def per_device(
    conv_in,
    gate_in,
    q_proj,
    k_proj,
    v_proj,
    conv_weight,
    conv_bias,
    proj_dt_weight,
    proj_bc_weight,
    dt_gain,
    dt_weight,
    dt_bias,
    decay_rate,
    skip_weight,
):
    tokens, channels = conv_in.shape
    span = WINDOW // tokens
    rank = dt_gain.shape[0]
    state_count = decay_rate.shape[0]
    blocks = channels // GROUP
    kv_here = k_proj.shape[1] // HD
    seq = lax.axis_size("seq")

    tail = shifted(conv_in[tokens - (KCONV - 1) :], "seq", 1)
    tail = jnp.pad(tail, ((TAIL - (KCONV - 1), 0), (0, 0)))
    own = jnp.concatenate([k_proj, v_proj], axis=1)
    pairs = [own] + [shifted(own, "seq", d) for d in range(1, span + 1)]
    position = lax.axis_index("seq").astype(jnp.int32).reshape(1)

    act, sums = project(
        tail, conv_in, conv_weight, conv_bias[None], proj_dt_weight, proj_bc_weight
    )
    if lax.axis_size("tp") == 2:
        sums = sums + lax.ppermute(sums, "tp", [(0, 1), (1, 0)])
    else:
        sums = lax.psum(sums, "tp")
    bc = sums[:, rank : rank + 2 * state_count].reshape(-1)
    rates = (
        (decay_rate * -LOG2E).reshape(state_count, blocks, SUBLANES, LANES).transpose(1, 0, 2, 3)
    )
    y, cum, state = local_scan(bc, sums, dt_gain[None], dt_weight, dt_bias[None], act, rates)
    span_time = cum[:, -SUBLANES:, :][:, None]

    def after(earlier, later):
        time_a, state_a = earlier
        time_b, state_b = later
        return time_a + time_b, jnp.exp2(rates * time_b) * state_a + state_b

    def fetch(value, steps):
        time, held = value
        time, held = shifted((time, held.astype(jnp.bfloat16)), "seq", steps)
        return time, held.astype(jnp.float32)

    value = (span_time, state)
    value = after(fetch(value, 2), fetch(value, 1))
    reach = 2
    while reach < seq - 1:
        value = after(fetch(value, reach), value)
        reach *= 2
    enter = value[1]

    attn_out = None
    for head in range(kv_here):
        attn_out = attention(head, position, q_proj, pairs, attn_out)
    mamba_out = finish(bc, y, cum, rates, enter, act, gate_in, skip_weight[None])
    return (mamba_out, attn_out)


def solution(mesh):
    return jax.shard_map(
        per_device,
        mesh=mesh,
        in_specs=(
            P("seq", "tp"),
            P("seq", "tp"),
            P("seq", "tp"),
            P("seq", "tp"),
            P("seq", "tp"),
            P(None, "tp"),
            P("tp"),
            P("tp", None),
            P(None, "tp"),
            P(),
            P(None, "tp"),
            P("tp"),
            P(None, "tp"),
            P("tp"),
        ),
        out_specs=(P("seq", "tp"), P("seq", "tp")),
        check_vma=False,
    )
```

profile of v0, /device:TPU:18, one launch (start us, length us, event | category | flops | bytes accessed | tf_op | source)
XLA Modules:
  0.0 301.5 jit_solution(12082626849943148764)
XLA Ops:
  1.6 3.4 %collective-permute-start = (bf16[3,8192]{1,0:T(4,128)(2,1)S(1)}, bf16[3,8192]{1,0:T(4,128)(2,1)S(1)}, u32[]{:S(2)}, u32[]{:S(2)}) collective-permute-start(bf16[3,8192]{1,0:T(4,128)(2,1)S(1)} %slice.9), channel_id=1, source_target_pairs={{0,2},{2,4},{4,6},{6,8},{8,10},{10,12},{12,14},{14,16},{16,18},{18... | collective-permute-start | bytes 147464 | tf_op jit(solution)/shard_map/ppermute | solution.py:25
  5.0 2.8 collective-permute-done
  8.5 14.5 %conv_and_projections.1 = (bf16[256,8192]{1,0:T(8,128)(2,1)}, f32[256,640]{1,0:T(8,128)}) custom-call(bf16[16,8192]{1,0:T(8,128)(2,1)} %pad.4.tail_ref, bf16[256,8192]{1,0:T(8,128)(2,1)} %x_ref.1, f32[4,8192]{1,0:T(4,128)} %taps_ref.1, f32[1,8192]{1,0:T(1,128)} %bitcast.49, bf16[8192,512]{1,0:T(8,128)(2,1)} %wdt_ref.2, bf16[32,8192]{1,0:T(8,128)(2,1)} %wbc_ref.1), custom_call_target="tpu_custom_call" | custom-call | flops 2281701376 | bytes 16777216 | tf_op jit(solution)/shard_map/conv_and_projections/pallas_call | solution.py:60
  23.2 4.4 %collective-permute-start.11 = (bf16[256,1024]{1,0:T(8,128)(2,1)S(1)}, bf16[256,1024]{1,0:T(8,128)(2,1)S(1)}, u32[]{:S(2)}, u32[]{:S(2)}) collective-permute-start(bf16[256,1024]{1,0:T(8,128)(2,1)S(1)} %constant_dynamic-update-slice_fusion.refs_2_.refs_11_), channel_id=1, source_target_pairs={{0,2},{2,4},{4,6},{6,8},{8,10},{10,12},{12,14},{14,16},{16,18},{18... | collective-permute-start | bytes 1572872 | tf_op jit(solution)/shard_map/ppermute | solution.py:25
  27.7 4.3 %collective-permute-start.12 = (bf16[256,1024]{1,0:T(8,128)(2,1)S(1)}, bf16[256,1024]{1,0:T(8,128)(2,1)S(1)}, u32[]{:S(2)}, u32[]{:S(2)}) collective-permute-start(bf16[256,1024]{1,0:T(8,128)(2,1)S(1)} %constant_dynamic-update-slice_fusion.refs_2_.refs_11_), channel_id=1, source_target_pairs={{0,4},{2,6},{4,8},{6,10},{8,12},{10,14},{12,16},{14,18},{16,20},{1... | collective-permute-start | bytes 1572872 | tf_op jit(solution)/shard_map/ppermute | solution.py:25
  33.9 1.9 collective-permute-start.14
  35.9 14.8 %collective-permute-done.11.refs_3_.refs_12_ = bf16[256,1024]{1,0:T(8,128)(2,1)S(1)} collective-permute-done((bf16[256,1024]{1,0:T(8,128)(2,1)S(1)}, bf16[256,1024]{1,0:T(8,128)(2,1)S(1)}, u32[]{:S(2)}, u32[]{:S(2)}) %collective-permute-start.11) | collective-permute-done | bytes 524320 | tf_op jit(solution)/shard_map/ppermute | solution.py:25
  50.6 6.3 %collective-permute-start.15 = (bf16[256,1024]{1,0:T(8,128)(2,1)S(1)}, bf16[256,1024]{1,0:T(8,128)(2,1)}, u32[]{:S(2)}, u32[]{:S(2)}) collective-permute-start(bf16[256,1024]{1,0:T(8,128)(2,1)S(1)} %constant_dynamic-update-slice_fusion.refs_2_.refs_11_), channel_id=1, source_target_pairs={{0,10},{2,12},{4,14},{6,16},{8,18},{10,20},{12,22},{14,24},{16,26}... | collective-permute-start | bytes 1572872 | tf_op jit(solution)/shard_map/ppermute | solution.py:25
  56.9 9.4 %collective-permute-done.12.refs_4_.refs_13_ = bf16[256,1024]{1,0:T(8,128)(2,1)S(1)} collective-permute-done((bf16[256,1024]{1,0:T(8,128)(2,1)S(1)}, bf16[256,1024]{1,0:T(8,128)(2,1)S(1)}, u32[]{:S(2)}, u32[]{:S(2)}) %collective-permute-start.12) | collective-permute-done | bytes 524320 | tf_op jit(solution)/shard_map/ppermute | solution.py:25
  68.2 3.1 %collective-permute-done.13.refs_5_.refs_14_ = bf16[256,1024]{1,0:T(8,128)(2,1)S(1)} collective-permute-done((bf16[256,1024]{1,0:T(8,128)(2,1)S(1)}, bf16[256,1024]{1,0:T(8,128)(2,1)S(1)}, u32[]{:S(2)}, u32[]{:S(2)}) %collective-permute-start.13) | collective-permute-done | bytes 524320 | tf_op jit(solution)/shard_map/ppermute | solution.py:25
  75.8 57.4 %local_scan.1 = (f32[8,2048,128]{2,1,0:T(8,128)}, f32[8,2048,128]{2,1,0:T(8,128)}, f32[8,16,8,128]{3,2,1,0:T(8,128)}) custom-call(f32[8192]{0:T(1024)} %reshape.13.bc_ref, f32[256,640]{1,0:T(8,128)} %copy-done, f32[1,512]{1,0:T(1,128)} %bitcast.52, bf16[512,8192]{1,0:T(8,128)(2,1)} %wdt_ref.3, f32[1,8192]{1,0:T(1,128)} %bitcast.50, ...), custom_call_target="tpu_custom_call" | custom-call | flops 2415919104 | bytes 33554432 | tf_op jit(solution)/shard_map/local_scan/pallas_call | solution.py:138
  135.1 8.3 %collective-permute-start.7 = (bf16[8,16,8,128]{3,2,1,0:T(8,128)(2,1)S(1)}, bf16[8,16,8,128]{3,2,1,0:T(8,128)(2,1)S(1)}, u32[]{:S(2)}, u32[]{:S(2)}) collective-permute-start(bf16[8,16,8,128]{3,2,1,0:T(8,128)(2,1)S(1)} %convert_element_type.30), channel_id=1, source_target_pairs={{0,2},{2,4},{4,6},{6,8},{8,10},{10,12},{12,14},{14,16},{16,18},{18... | collective-permute-start | bytes 786440 | tf_op jit(solution)/shard_map/ppermute | solution.py:25
  143.4 1.9 collective-permute-start.6
  145.4 7.4 %collective-permute-start.3 = (f32[8,1,8,128]{3,2,0,1:T(8,128)S(1)}, f32[8,1,8,128]{3,2,0,1:T(8,128)S(1)}, u32[]{:S(2)}, u32[]{:S(2)}) collective-permute-start(f32[8,1,8,128]{3,2,0,1:T(8,128)S(1)} %slice_bitcast_fusion), channel_id=1, source_target_pairs={{0,2},{2,4},{4,6},{6,8},{8,10},{10,12},{12,14},{14,16},{16,18},{18... | collective-permute-start | bytes 98312 | tf_op jit(solution)/shard_map/ppermute | solution.py:25
  152.9 15.4 %window_attention.4.refs_20_ = bf16[256,4096]{1,0:T(8,128)(2,1)} custom-call(s32[1]{0:T(128)} %bitcast.10.refs_0_, bf16[256,4096]{1,0:T(8,128)(2,1)} %refs_1_.7, bf16[256,1024]{1,0:T(8,128)(2,1)} %copy-done.5, bf16[256,1024]{1,0:T(8,128)(2,1)} %copy-done.6, bf16[256,1024]{1,0:T(8,128)(2,1)} %copy-done.7, bf16[256,1024]{1,0:T(8,128)(2,1)} %copy-done.8, ...), custom_call_target="tpu_custom_call" | custom-call | flops 4831838208 | bytes 2228224 | tf_op jit(solution)/shard_map/window_attention/pallas_call | solution.py:301
  170.2 24.4 %collective-permute-done.6 = bf16[8,16,8,128]{3,2,1,0:T(8,128)(2,1)S(1)} collective-permute-done((bf16[8,16,8,128]{3,2,1,0:T(8,128)(2,1)S(1)}, bf16[8,16,8,128]{3,2,1,0:T(8,128)(2,1)S(1)}, u32[]{:S(2)}, u32[]{:S(2)}) %collective-permute-start.6) | collective-permute-done | bytes 262176 | tf_op jit(solution)/shard_map/ppermute | solution.py:25
  194.8 1.9 collective-permute-start.8
  196.7 15.5 %window_attention.5.refs_20_ = bf16[256,4096]{1,0:T(8,128)(2,1)} custom-call(s32[1]{0:T(128)} %bitcast.10.refs_0_, bf16[256,4096]{1,0:T(8,128)(2,1)} %refs_1_.7, bf16[256,1024]{1,0:T(8,128)(2,1)} %copy-done.5, bf16[256,1024]{1,0:T(8,128)(2,1)} %copy-done.6, bf16[256,1024]{1,0:T(8,128)(2,1)} %copy-done.7, ...), custom_call_target="tpu_custom_call", output_to_operand_aliasing={{}: (20, {})} | custom-call | flops 4831838208 | bytes 2228224 | tf_op jit(solution)/shard_map/window_attention/pallas_call | solution.py:301
  212.2 11.8 %collective-permute-start.4 = (f32[8,1,8,128]{3,2,0,1:T(8,128)S(1)}, f32[8,1,8,128]{3,2,0,1:T(8,128)S(1)}, u32[]{:S(2)}, u32[]{:S(2)}) collective-permute-start(f32[8,1,8,128]{3,2,0,1:T(8,128)S(1)} %add.27), channel_id=1, source_target_pairs={{0,4},{2,6},{4,8},{6,10},{8,12},{10,14},{12,16},{14,18},{16,20},{1... | collective-permute-start | bytes 98312 | tf_op jit(solution)/shard_map/ppermute | solution.py:25
  224.3 1.9 collective-permute-start.9
  226.3 15.5 %window_attention.6.refs_20_ = bf16[256,4096]{1,0:T(8,128)(2,1)} custom-call(s32[1]{0:T(128)} %bitcast.10.refs_0_, bf16[256,4096]{1,0:T(8,128)(2,1)} %refs_1_.7, bf16[256,1024]{1,0:T(8,128)(2,1)} %copy-done.5, bf16[256,1024]{1,0:T(8,128)(2,1)} %copy-done.6, bf16[256,1024]{1,0:T(8,128)(2,1)} %copy-done.7, ...), custom_call_target="tpu_custom_call", output_to_operand_aliasing={{}: (20, {})} | custom-call | flops 4831838208 | bytes 2228224 | tf_op jit(solution)/shard_map/window_attention/pallas_call | solution.py:301
  241.7 1.9 collective-permute-start.5
  245.6 15.5 %window_attention.7 = bf16[256,4096]{1,0:T(8,128)(2,1)} custom-call(s32[1]{0:T(128)} %bitcast.10.refs_0_, bf16[256,4096]{1,0:T(8,128)(2,1)} %refs_1_.7, bf16[256,1024]{1,0:T(8,128)(2,1)} %copy-done.5, bf16[256,1024]{1,0:T(8,128)(2,1)} %copy-done.6, bf16[256,1024]{1,0:T(8,128)(2,1)} %copy-done.7, ...), custom_call_target="tpu_custom_call", output_to_operand_aliasing={{}: (20, {})} | custom-call | flops 4831838208 | bytes 2228224 | tf_op jit(solution)/shard_map/window_attention/pallas_call | solution.py:301
  262.4 39.1 %carry_and_gate.1 = bf16[256,8192]{1,0:T(8,128)(2,1)} custom-call(f32[8192]{0:T(1024)} %reshape.13.bc_ref, f32[8,2048,128]{2,1,0:T(8,128)} %get-tuple-element.9.y_ref, f32[8,2048,128]{2,1,0:T(8,128)} %get-tuple-element.10.cum_ref, f32[8,16,8,128]{3,2,1,0:T(8,128)} %bitcast.48, f32[8,16,8,128]{3,2,1,0:T(8,128)} %multiply_add_fusion.enter_ref, ...), custom_call_target="tpu_custom_call" | custom-call | flops 201326592 | bytes 29360128 | tf_op jit(solution)/shard_map/carry_and_gate/pallas_call | solution.py:202
  (58 shorter events, 17.6 us)
Async XLA Ops:
  1.6 6.2 %collective-permute-start = (bf16[3,8192]{1,0:T(4,128)(2,1)S(1)}, bf16[3,8192]{1,0:T(4,128)(2,1)S(1)}, u32[]{:S(2)}, u32[]{:S(2)}) collective-permute-start(bf16[3,8192]{1,0:T(4,128)(2,1)S(1)} %slice.9), channel_id=1, source_target_pairs={{0,2},{2,4},{4,6},{6,8},{8,10},{10,12},{12,14},{14,16},{16,18},{18... | collective-permute-start | bytes 147464 | tf_op jit(solution)/shard_map/ppermute | solution.py:25
  8.5 14.7 %copy-start.4 = (bf16[256,512]{1,0:T(8,128)(2,1)S(1)}, bf16[256,512]{1,0:T(8,128)(2,1)}, u32[]{:S(2)}) copy-start(bf16[256,512]{1,0:T(8,128)(2,1)} %param.18) | copy-start | bytes 786436
  8.5 65.4 %copy-start.2 = (f32[16,8192]{1,0:T(8,128)S(1)}, f32[16,8192]{1,0:T(8,128)}, u32[]{:S(2)}) copy-start(f32[16,8192]{1,0:T(8,128)} %param.26) | copy-start | bytes 1572868
  23.0 51.9 %copy-start.1 = (f32[256,640]{1,0:T(8,128)S(1)}, f32[256,640]{1,0:T(8,128)}, u32[]{:S(2)}) copy-start(f32[256,640]{1,0:T(8,128)} %get-tuple-element.7) | copy-start | bytes 1966084
  23.0 49.5 %collective-permute-start.1 = (f32[256,640]{1,0:T(8,128)}, f32[256,640]{1,0:T(8,128)S(1)}, u32[]{:S(2)}, u32[]{:S(2)}) collective-permute-start(f32[256,640]{1,0:T(8,128)} %get-tuple-element.7), channel_id=1, source_target_pairs={{0,1},{1,0},{2,3},{3,2},{4,5},{5,4},{6,7},{7,6},{8,9},{9,8},{10,11... | collective-permute-start | bytes 1966088 | tf_op jit(solution)/shard_map/ppermute | solution.py:357
  23.2 110.0 %copy-start.5 = (bf16[256,1024]{1,0:T(8,128)(2,1)}, bf16[256,1024]{1,0:T(8,128)(2,1)S(1)}, u32[]{:S(2)}) copy-start(bf16[256,1024]{1,0:T(8,128)(2,1)S(1)} %constant_dynamic-update-slice_fusion.refs_2_.refs_11_) | copy-start | bytes 1572868
  23.2 27.4 %collective-permute-start.11 = (bf16[256,1024]{1,0:T(8,128)(2,1)S(1)}, bf16[256,1024]{1,0:T(8,128)(2,1)S(1)}, u32[]{:S(2)}, u32[]{:S(2)}) collective-permute-start(bf16[256,1024]{1,0:T(8,128)(2,1)S(1)} %constant_dynamic-update-slice_fusion.refs_2_.refs_11_), channel_id=1, source_target_pairs={{0,2},{2,4},{4,6},{6,8},{8,10},{10,12},{12,14},{14,16},{16,18},{18... | collective-permute-start | bytes 1572872 | tf_op jit(solution)/shard_map/ppermute | solution.py:25
  27.7 38.6 %collective-permute-start.12 = (bf16[256,1024]{1,0:T(8,128)(2,1)S(1)}, bf16[256,1024]{1,0:T(8,128)(2,1)S(1)}, u32[]{:S(2)}, u32[]{:S(2)}) collective-permute-start(bf16[256,1024]{1,0:T(8,128)(2,1)S(1)} %constant_dynamic-update-slice_fusion.refs_2_.refs_11_), channel_id=1, source_target_pairs={{0,4},{2,6},{4,8},{6,10},{8,12},{10,14},{12,16},{14,18},{16,20},{1... | collective-permute-start | bytes 1572872 | tf_op jit(solution)/shard_map/ppermute | solution.py:25
  32.0 39.3 %collective-permute-start.13 = (bf16[256,1024]{1,0:T(8,128)(2,1)S(1)}, bf16[256,1024]{1,0:T(8,128)(2,1)S(1)}, u32[]{:S(2)}, u32[]{:S(2)}) collective-permute-start(bf16[256,1024]{1,0:T(8,128)(2,1)S(1)} %constant_dynamic-update-slice_fusion.refs_2_.refs_11_), channel_id=1, source_target_pairs={{0,6},{2,8},{4,10},{6,12},{8,14},{10,16},{12,18},{14,20},{16,22},{... | collective-permute-start | bytes 1572872 | tf_op jit(solution)/shard_map/ppermute | solution.py:25
  33.9 101.2 %collective-permute-start.14 = (bf16[256,1024]{1,0:T(8,128)(2,1)S(1)}, bf16[256,1024]{1,0:T(8,128)(2,1)}, u32[]{:S(2)}, u32[]{:S(2)}) collective-permute-start(bf16[256,1024]{1,0:T(8,128)(2,1)S(1)} %constant_dynamic-update-slice_fusion.refs_2_.refs_11_), channel_id=1, source_target_pairs={{0,8},{2,10},{4,12},{6,14},{8,16},{10,18},{12,20},{14,22},{16,24},... | collective-permute-start | bytes 1572872 | tf_op jit(solution)/shard_map/ppermute | solution.py:25
  50.6 82.6 %copy-start.6 = (bf16[256,1024]{1,0:T(8,128)(2,1)}, bf16[256,1024]{1,0:T(8,128)(2,1)S(1)}, u32[]{:S(2)}) copy-start(bf16[256,1024]{1,0:T(8,128)(2,1)S(1)} %collective-permute-done.11.refs_3_.refs_12_) | copy-start | bytes 1572868
  50.6 92.8 %collective-permute-start.15 = (bf16[256,1024]{1,0:T(8,128)(2,1)S(1)}, bf16[256,1024]{1,0:T(8,128)(2,1)}, u32[]{:S(2)}, u32[]{:S(2)}) collective-permute-start(bf16[256,1024]{1,0:T(8,128)(2,1)S(1)} %constant_dynamic-update-slice_fusion.refs_2_.refs_11_), channel_id=1, source_target_pairs={{0,10},{2,12},{4,14},{6,16},{8,18},{10,20},{12,22},{14,24},{16,26}... | collective-permute-start | bytes 1572872 | tf_op jit(solution)/shard_map/ppermute | solution.py:25
  66.3 79.1 %collective-permute-start.16 = (bf16[256,1024]{1,0:T(8,128)(2,1)S(1)}, bf16[256,1024]{1,0:T(8,128)(2,1)}, u32[]{:S(2)}, u32[]{:S(2)}) collective-permute-start(bf16[256,1024]{1,0:T(8,128)(2,1)S(1)} %constant_dynamic-update-slice_fusion.refs_2_.refs_11_), channel_id=1, source_target_pairs={{0,12},{2,14},{4,16},{6,18},{8,20},{10,22},{12,24},{14,26},{16,28}... | collective-permute-start | bytes 1572872 | tf_op jit(solution)/shard_map/ppermute | solution.py:25
  71.3 81.5 %collective-permute-start.17 = (bf16[256,1024]{1,0:T(8,128)(2,1)S(1)}, bf16[256,1024]{1,0:T(8,128)(2,1)}, u32[]{:S(2)}, u32[]{:S(2)}) collective-permute-start(bf16[256,1024]{1,0:T(8,128)(2,1)S(1)} %constant_dynamic-update-slice_fusion.refs_2_.refs_11_), channel_id=1, source_target_pairs={{0,14},{2,16},{4,18},{6,20},{8,22},{10,24},{12,26},{14,28},{16,30}... | collective-permute-start | bytes 1572872 | tf_op jit(solution)/shard_map/ppermute | solution.py:25
  72.6 80.2 %collective-permute-start.18 = (bf16[256,1024]{1,0:T(8,128)(2,1)S(1)}, bf16[256,1024]{1,0:T(8,128)(2,1)}, u32[]{:S(2)}, u32[]{:S(2)}) collective-permute-start(bf16[256,1024]{1,0:T(8,128)(2,1)S(1)} %constant_dynamic-update-slice_fusion.refs_2_.refs_11_), channel_id=1, source_target_pairs={{0,16},{2,18},{4,20},{6,22},{8,24},{10,26},{12,28},{14,30},{1,17},... | collective-permute-start | bytes 1572872 | tf_op jit(solution)/shard_map/ppermute | solution.py:25
  135.1 35.1 %collective-permute-start.7 = (bf16[8,16,8,128]{3,2,1,0:T(8,128)(2,1)S(1)}, bf16[8,16,8,128]{3,2,1,0:T(8,128)(2,1)S(1)}, u32[]{:S(2)}, u32[]{:S(2)}) collective-permute-start(bf16[8,16,8,128]{3,2,1,0:T(8,128)(2,1)S(1)} %convert_element_type.30), channel_id=1, source_target_pairs={{0,2},{2,4},{4,6},{6,8},{8,10},{10,12},{12,14},{14,16},{16,18},{18... | collective-permute-start | bytes 786440 | tf_op jit(solution)/shard_map/ppermute | solution.py:25
  143.4 51.1 %collective-permute-start.6 = (bf16[8,16,8,128]{3,2,1,0:T(8,128)(2,1)S(1)}, bf16[8,16,8,128]{3,2,1,0:T(8,128)(2,1)S(1)}, u32[]{:S(2)}, u32[]{:S(2)}) collective-permute-start(bf16[8,16,8,128]{3,2,1,0:T(8,128)(2,1)S(1)} %convert_element_type.30), channel_id=1, source_target_pairs={{0,4},{2,6},{4,8},{6,10},{8,12},{10,14},{12,16},{14,18},{16,20},{1... | collective-permute-start | bytes 786440 | tf_op jit(solution)/shard_map/ppermute | solution.py:25
  145.4 24.8 %collective-permute-start.3 = (f32[8,1,8,128]{3,2,0,1:T(8,128)S(1)}, f32[8,1,8,128]{3,2,0,1:T(8,128)S(1)}, u32[]{:S(2)}, u32[]{:S(2)}) collective-permute-start(f32[8,1,8,128]{3,2,0,1:T(8,128)S(1)} %slice_bitcast_fusion), channel_id=1, source_target_pairs={{0,2},{2,4},{4,6},{6,8},{8,10},{10,12},{12,14},{14,16},{16,18},{18... | collective-permute-start | bytes 98312 | tf_op jit(solution)/shard_map/ppermute | solution.py:25
  168.3 43.9 %collective-permute-start.2 = (f32[8,1,8,128]{3,2,0,1:T(8,128)S(1)}, f32[8,1,8,128]{3,2,0,1:T(8,128)S(1)}, u32[]{:S(2)}, u32[]{:S(2)}) collective-permute-start(f32[8,1,8,128]{3,2,0,1:T(8,128)S(1)} %slice_bitcast_fusion), channel_id=1, source_target_pairs={{0,4},{2,6},{4,8},{6,10},{8,12},{10,14},{12,16},{14,18},{16,20},{1... | collective-permute-start | bytes 98312 | tf_op jit(solution)/shard_map/ppermute | solution.py:25
  194.8 29.3 %collective-permute-start.8 = (bf16[8,16,8,128]{3,2,1,0:T(8,128)(2,1)S(1)}, bf16[8,16,8,128]{3,2,1,0:T(8,128)(2,1)S(1)}, u32[]{:S(2)}, u32[]{:S(2)}) collective-permute-start(bf16[8,16,8,128]{3,2,1,0:T(8,128)(2,1)S(1)} %fusion), channel_id=1, source_target_pairs={{0,4},{2,6},{4,8},{6,10},{8,12},{10,14},{12,16},{14,18},{16,20},{1... | collective-permute-start | bytes 786440 | tf_op jit(solution)/shard_map/ppermute | solution.py:25
  212.2 29.5 %collective-permute-start.4 = (f32[8,1,8,128]{3,2,0,1:T(8,128)S(1)}, f32[8,1,8,128]{3,2,0,1:T(8,128)S(1)}, u32[]{:S(2)}, u32[]{:S(2)}) collective-permute-start(f32[8,1,8,128]{3,2,0,1:T(8,128)S(1)} %add.27), channel_id=1, source_target_pairs={{0,4},{2,6},{4,8},{6,10},{8,12},{10,14},{12,16},{14,18},{16,20},{1... | collective-permute-start | bytes 98312 | tf_op jit(solution)/shard_map/ppermute | solution.py:25
  224.3 19.4 %collective-permute-start.9 = (bf16[8,16,8,128]{3,2,1,0:T(8,128)(2,1)S(1)}, bf16[8,16,8,128]{3,2,1,0:T(8,128)(2,1)S(1)}, u32[]{:S(2)}, u32[]{:S(2)}) collective-permute-start(bf16[8,16,8,128]{3,2,1,0:T(8,128)(2,1)S(1)} %fusion.2), channel_id=1, source_target_pairs={{0,8},{2,10},{4,12},{6,14},{8,16},{10,18},{12,20},{14,22},{16,24},... | collective-permute-start | bytes 786440 | tf_op jit(solution)/shard_map/ppermute | solution.py:25
  241.7 19.3 %collective-permute-start.5 = (f32[8,1,8,128]{3,2,0,1:T(8,128)S(1)}, f32[8,1,8,128]{3,2,0,1:T(8,128)S(1)}, u32[]{:S(2)}, u32[]{:S(2)}) collective-permute-start(f32[8,1,8,128]{3,2,0,1:T(8,128)S(1)} %add.28), channel_id=1, source_target_pairs={{0,8},{2,10},{4,12},{6,14},{8,16},{10,18},{12,20},{14,22},{16,24},... | collective-permute-start | bytes 98312 | tf_op jit(solution)/shard_map/ppermute | solution.py:25
  244.1 17.0 %collective-permute-start.10 = (bf16[8,16,8,128]{3,2,1,0:T(8,128)(2,1)S(1)}, bf16[8,16,8,128]{3,2,1,0:T(8,128)(2,1)S(1)}, u32[]{:S(2)}, u32[]{:S(2)}) collective-permute-start(bf16[8,16,8,128]{3,2,1,0:T(8,128)(2,1)S(1)} %fusion.1), channel_id=1, source_target_pairs={{0,16},{2,18},{4,20},{6,22},{8,24},{10,26},{12,28},{14,30},{1,17},... | collective-permute-start | bytes 786440 | tf_op jit(solution)/shard_map/ppermute | solution.py:25
  (4 other events, 25.4 us)
where the time goes:
time: 306 us; the launch traced here: 301 us
  Pallas kernels  173 us (57%)
  starting transfers between devices  65.5 us (21%)
  waiting for transfers between devices  54.4 us (18%)
  local copies, waits for them, and re-layouts  4.3 us (1%)
  other arithmetic  3.37 us (1%)
    ppermute x18, starting transfers between devices, shifted(): lax.ppermute(value, axis, [(source, source + steps) for source in range(c...  65.5 us
    pallas_call x4, Pallas kernels, attention(): pl.pallas_call(functools.partial(attention_kernel, span, aliased), grid=(...  61.9 us
    pallas_call x1, Pallas kernels, local_scan(): pl.pallas_call(functools.partial(scan_kernel, rank, state_count), grid=(b...  57.4 us
    ppermute x18, waiting for transfers between devices, shifted(): lax.ppermute(value, axis, [(source, source + steps) for source in range(c...  54.4 us
    pallas_call x1, Pallas kernels, finish(): pl.pallas_call(functools.partial(finish_kernel, state_count), grid=(block...  39.1 us
    pallas_call x1, Pallas kernels, project(): pl.pallas_call(functools.partial(project_kernel, rank), grid=(blocks,), i...  14.5 us
  transfers between devices with their start and end apart: 19, of which 5 were waited for; matrix products, arithmetic and copies ran while one was open for 2% of the time, Pallas kernels for 40%

commit v1 on v0

v1 whole, which is shorter than its diff:
```python
import functools
import math

import jax
import jax.numpy as jnp
from jax import lax
from jax.experimental import pallas as pl
from jax.experimental.pallas import tpu as pltpu
from jax.sharding import PartitionSpec as P

KCONV = 4
HD = 128
WINDOW = 2048
LANES = 128
SUBLANES = 8
GROUP = LANES * SUBLANES
TAIL = 16
LOG2E = math.log2(math.e)
FAR = -1e30
epsilon = 1e-06


def shifted(value, axis, steps):
    count = lax.axis_size(axis)
    return lax.ppermute(value, axis, [(source, source + steps) for source in range(count - steps)])


def params(mib=56):
    return pltpu.CompilerParams(vmem_limit_bytes=mib * 1024 * 1024)


def project_kernel(rank, tail_ref, x_ref, taps_ref, bias_ref, wdt_ref, wbc_ref, act_ref, sums_ref, wide):
    tokens = x_ref.shape[0]
    wide[:TAIL] = tail_ref[...].astype(jnp.float32)
    wide[TAIL:] = x_ref[...].astype(jnp.float32)
    total = bias_ref[...] + taps_ref[0:1] * wide[pl.ds(TAIL - 3, tokens)]
    for j in range(1, KCONV):
        total = total + taps_ref[j : j + 1] * wide[pl.ds(TAIL - 3 + j, tokens)]
    act = (total / (1.0 + jnp.exp(-total))).astype(jnp.bfloat16)
    act_ref[...] = act
    low = jnp.dot(act, wdt_ref[...], preferred_element_type=jnp.float32)
    state = lax.dot_general(
        act, wbc_ref[...], (((1,), (1,)), ((), ())), preferred_element_type=jnp.float32
    )
    states = state.shape[1]

    @pl.when(pl.program_id(0) == 0)
    def _():
        sums_ref[...] = jnp.zeros_like(sums_ref)

    sums_ref[:, :rank] += low
    sums_ref[:, rank : rank + states] += state


def project(tail, conv_in, taps, bias, wdt, wbc):
    tokens, channels = conv_in.shape
    rank = wdt.shape[1]
    states = wbc.shape[0]
    blocks = channels // GROUP
    return pl.pallas_call(
        functools.partial(project_kernel, rank),
        grid=(blocks,),
        in_specs=[
            pl.BlockSpec((TAIL, GROUP), lambda i: (0, i)),
            pl.BlockSpec((tokens, GROUP), lambda i: (0, i)),
            pl.BlockSpec((KCONV, GROUP), lambda i: (0, i)),
            pl.BlockSpec((1, GROUP), lambda i: (0, i)),
            pl.BlockSpec((GROUP, rank), lambda i: (i, 0)),
            pl.BlockSpec((states, GROUP), lambda i: (0, i)),
        ],
        out_specs=[
            pl.BlockSpec((tokens, GROUP), lambda i: (0, i)),
            pl.BlockSpec((tokens, rank + LANES), lambda i: (0, 0)),
        ],
        out_shape=[
            jax.ShapeDtypeStruct((tokens, channels), jnp.bfloat16),
            jax.ShapeDtypeStruct((tokens, rank + LANES), jnp.float32),
        ],
        scratch_shapes=[pltpu.VMEM((TAIL + tokens, GROUP), jnp.float32)],
        compiler_params=params(),
        cost_estimate=pl.CostEstimate(
            flops=2 * tokens * channels * (rank + states),
            bytes_accessed=4 * tokens * channels + 2 * channels * rank,
            transcendentals=tokens * channels,
        ),
        name="conv_and_projections",
    )(tail, conv_in, taps, bias, wdt, wbc)


def scan_kernel(rank, state_count, bc_ref, low_ref, gain_ref, wdt_ref, bias_ref, act_ref, rate_ref,
                y_ref, cum_ref, packed_ref, normed, steps, drives):
    tokens = act_ref.shape[0]
    pair = rate_ref.shape[0]

    @pl.when(pl.program_id(0) == 0)
    def _():
        low = low_ref[:, :rank]
        mean_square = jnp.mean(low * low, axis=-1, keepdims=True)
        normed[...] = (low * lax.rsqrt(mean_square + epsilon) * gain_ref[...]).astype(jnp.bfloat16)

    for j in range(pair * SUBLANES):
        cols = slice(j * LANES, (j + 1) * LANES)
        where = pl.ds(j % SUBLANES, tokens, stride=SUBLANES)
        raw = (
            jnp.dot(normed[...], wdt_ref[:, cols], preferred_element_type=jnp.float32)
            + bias_ref[:, cols]
        )
        step = jnp.maximum(raw, 0.0) + jnp.log1p(jnp.exp(-jnp.abs(raw)))
        steps[j // SUBLANES, where, :] = step
        drives[j // SUBLANES, where, :] = step * act_ref[:, cols].astype(jnp.float32)

    def advance(t, carry):
        through, hidden = carry
        rows = pl.ds(pl.multiple_of(t * SUBLANES, SUBLANES), SUBLANES)
        step = [steps[p, rows, :] for p in range(pair)]
        drive = [drives[p, rows, :] for p in range(pair)]
        base = t * (2 * state_count)
        out = [None] * pair
        new = []
        for n in range(state_count):
            into, onto = bc_ref[base + n], bc_ref[base + state_count + n]
            for p in range(pair):
                h = jnp.exp2(rate_ref[p, n] * step[p]) * hidden[n * pair + p] + into * drive[p]
                out[p] = onto * h if n == 0 else out[p] + onto * h
                new.append(h)
        through = tuple(through[p] + step[p] for p in range(pair))
        for p in range(pair):
            y_ref[p, rows, :] = out[p]
            cum_ref[p, rows, :] = through[p]
        return through, tuple(new)

    zero = jnp.zeros((SUBLANES, LANES), jnp.float32)
    through, hidden = lax.fori_loop(
        0, tokens, advance, ((zero,) * pair, (zero,) * (state_count * pair)), unroll=2
    )
    size = 2 * SUBLANES
    for p in range(pair):
        for n in range(0, state_count, 2):
            both = jnp.concatenate([hidden[n * pair + p], hidden[(n + 1) * pair + p]], axis=0)
            packed_ref[p, n // 2 * size : (n // 2 + 1) * size] = both.astype(jnp.bfloat16)
        high = through[p].astype(jnp.bfloat16).astype(jnp.float32)
        middle = (through[p] - high).astype(jnp.bfloat16).astype(jnp.float32)
        low = through[p] - high - middle
        first = state_count // 2 * size
        packed_ref[p, first : first + size] = jnp.concatenate([high, middle], axis=0).astype(
            jnp.bfloat16
        )
        packed_ref[p, first + size : first + 2 * size] = jnp.concatenate([low, zero], axis=0).astype(
            jnp.bfloat16
        )


def local_scan(bc, low, gain, wdt, bias, act, rates):
    tokens, channels = act.shape
    rank = gain.shape[1]
    blocks, state_count = rates.shape[:2]
    rows = tokens * SUBLANES
    pair = 2 if blocks % 2 == 0 else 1
    width = pair * GROUP
    packed = (state_count + 4) * SUBLANES
    return pl.pallas_call(
        functools.partial(scan_kernel, rank, state_count),
        grid=(blocks // pair,),
        in_specs=[
            pl.BlockSpec(memory_space=pltpu.SMEM),
            pl.BlockSpec(low.shape, lambda i: (0, 0)),
            pl.BlockSpec((1, rank), lambda i: (0, 0)),
            pl.BlockSpec((rank, width), lambda i: (0, i)),
            pl.BlockSpec((1, width), lambda i: (0, i)),
            pl.BlockSpec((tokens, width), lambda i: (0, i)),
            pl.BlockSpec((pair, state_count, SUBLANES, LANES), lambda i: (i, 0, 0, 0)),
        ],
        out_specs=[
            pl.BlockSpec((pair, rows, LANES), lambda i: (i, 0, 0)),
            pl.BlockSpec((pair, rows, LANES), lambda i: (i, 0, 0)),
            pl.BlockSpec((pair, packed, LANES), lambda i: (i, 0, 0)),
        ],
        out_shape=[
            jax.ShapeDtypeStruct((blocks, rows, LANES), jnp.float32),
            jax.ShapeDtypeStruct((blocks, rows, LANES), jnp.float32),
            jax.ShapeDtypeStruct((blocks, packed, LANES), jnp.bfloat16),
        ],
        scratch_shapes=[
            pltpu.VMEM((tokens, rank), jnp.bfloat16),
            pltpu.VMEM((pair, rows, LANES), jnp.float32),
            pltpu.VMEM((pair, rows, LANES), jnp.float32),
        ],
        compiler_params=params(),
        cost_estimate=pl.CostEstimate(
            flops=2 * tokens * channels * rank + 8 * tokens * channels * state_count,
            bytes_accessed=12 * tokens * channels + 2 * channels * rank,
            transcendentals=tokens * channels * state_count,
        ),
        name="local_scan",
    )(bc, low, gain, wdt, bias, act, rates)


TOKENS_AT_ONCE = 4


def finish_kernel(state_count, position, bc_ref, y_ref, cum_ref, rate_ref, all_ref, act_ref, gate_ref,
                  skip_ref, out_ref, mixed, enter):
    tokens = act_ref.shape[0]
    pair = rate_ref.shape[0]
    size = 2 * SUBLANES
    halves = state_count // 2
    for p in range(pair):

        def compose(k, held):
            parts = all_ref[k, p, halves * size : (halves + 2) * size].astype(jnp.float32)
            span = (
                parts[:SUBLANES]
                + parts[SUBLANES : 2 * SUBLANES]
                + parts[2 * SUBLANES : 3 * SUBLANES]
            )
            new = []
            for n in range(state_count):
                if n % 2 == 0:
                    both = all_ref[k, p, n // 2 * size : (n // 2 + 1) * size].astype(jnp.float32)
                own = both[n % 2 * SUBLANES : (n % 2 + 1) * SUBLANES]
                new.append(jnp.exp2(rate_ref[p, n] * span) * held[n] + own)
            return tuple(new)

        zero = jnp.zeros((SUBLANES, LANES), jnp.float32)
        held = lax.fori_loop(0, position[0], compose, (zero,) * state_count)
        for n in range(state_count):
            enter[p, n] = held[n]

    def adjust(step, carry):
        first = step * TOKENS_AT_ONCE
        rows = [
            pl.ds(pl.multiple_of((first + u) * SUBLANES, SUBLANES), SUBLANES)
            for u in range(TOKENS_AT_ONCE)
        ]
        through = [[cum_ref[p, r, :] for r in rows] for p in range(pair)]
        total = [[y_ref[p, r, :] for r in rows] for p in range(pair)]
        base = first * (2 * state_count) + state_count
        for n in range(state_count):
            onto = [bc_ref[base + u * (2 * state_count) + n] for u in range(TOKENS_AT_ONCE)]
            for p in range(pair):
                rate, held = rate_ref[p, n], enter[p, n]
                for u in range(TOKENS_AT_ONCE):
                    total[p][u] = total[p][u] + onto[u] * (jnp.exp2(rate * through[p][u]) * held)
        for p in range(pair):
            for u in range(TOKENS_AT_ONCE):
                mixed[p, rows[u], :] = total[p][u]
        return carry

    lax.fori_loop(0, tokens // TOKENS_AT_ONCE, adjust, 0)
    for j in range(pair * SUBLANES):
        cols = slice(j * LANES, (j + 1) * LANES)
        gate = gate_ref[:, cols].astype(jnp.float32)
        value = mixed[j // SUBLANES, pl.ds(j % SUBLANES, tokens, stride=SUBLANES), :]
        value = value + skip_ref[:, cols] * act_ref[:, cols].astype(jnp.float32)
        out_ref[:, cols] = (value * (gate / (1.0 + jnp.exp(-gate)))).astype(jnp.bfloat16)


def finish(position, bc, y, cum, rates, everything, act, gate, skip):
    tokens, channels = act.shape
    blocks, state_count = rates.shape[:2]
    rows = tokens * SUBLANES
    pair = 2 if blocks % 2 == 0 else 1
    width = pair * GROUP
    peers, _, packed, _ = everything.shape
    return pl.pallas_call(
        functools.partial(finish_kernel, state_count),
        grid=(blocks // pair,),
        in_specs=[
            pl.BlockSpec(memory_space=pltpu.SMEM),
            pl.BlockSpec(memory_space=pltpu.SMEM),
            pl.BlockSpec((pair, rows, LANES), lambda i: (i, 0, 0)),
            pl.BlockSpec((pair, rows, LANES), lambda i: (i, 0, 0)),
            pl.BlockSpec((pair, state_count, SUBLANES, LANES), lambda i: (i, 0, 0, 0)),
            pl.BlockSpec((peers, pair, packed, LANES), lambda i: (0, i, 0, 0)),
            pl.BlockSpec((tokens, width), lambda i: (0, i)),
            pl.BlockSpec((tokens, width), lambda i: (0, i)),
            pl.BlockSpec((1, width), lambda i: (0, i)),
        ],
        out_specs=pl.BlockSpec((tokens, width), lambda i: (0, i)),
        out_shape=jax.ShapeDtypeStruct((tokens, channels), jnp.bfloat16),
        scratch_shapes=[
            pltpu.VMEM((pair, rows, LANES), jnp.float32),
            pltpu.VMEM((pair, state_count, SUBLANES, LANES), jnp.float32),
        ],
        compiler_params=params(),
        cost_estimate=pl.CostEstimate(
            flops=6 * tokens * channels * state_count,
            bytes_accessed=14 * tokens * channels,
            transcendentals=tokens * channels * state_count,
        ),
        name="carry_and_gate",
    )(position, bc, y, cum, rates, everything, act, gate, skip)


def attention_kernel(span, position, q_ref, *refs):
    key_refs = refs[: 1 + span]
    value_refs = refs[1 + span : 2 + 2 * span]
    out_ref, keys, values, scores = refs[2 + 2 * span :]
    tokens = q_ref.shape[0]

    @pl.when(pl.program_id(1) == 0)
    def _():
        first = lax.broadcasted_iota(jnp.int32, (tokens, HD), 1) == 0
        for d in range(span + 1):
            rows = slice(d * tokens, (d + 1) * tokens)
            absent = jnp.where(position[0] >= d, 0.0, FAR)
            keys[rows, :HD] = key_refs[d][0]
            keys[rows, HD:] = jnp.where(first, absent, 0.0).astype(jnp.bfloat16)
            values[rows, :HD] = value_refs[d][0]
            values[rows, HD:] = jnp.ones((tokens, HD), jnp.bfloat16)

    ones = (lax.broadcasted_iota(jnp.int32, (tokens, HD), 1) == 0).astype(jnp.bfloat16)
    query = jnp.concatenate([q_ref[...], ones], axis=1)
    near = lax.broadcasted_iota(jnp.int32, (tokens, tokens), 1) <= lax.broadcasted_iota(
        jnp.int32, (tokens, tokens), 0
    )

    def score(d):
        return lax.dot_general(
            query,
            keys[d * tokens : (d + 1) * tokens],
            (((1,), (1,)), ((), ())),
            preferred_element_type=jnp.float32,
        )

    block = jnp.where(near, score(0), score(span))
    scores[0] = block
    peak = block
    for d in range(1, span):
        block = score(d)
        scores[d] = block
        peak = jnp.maximum(peak, block)
    factor = LOG2E / math.sqrt(HD)
    peak = jnp.max(peak, axis=-1, keepdims=True) * factor
    weight = jnp.exp2(scores[0] * factor - peak).astype(jnp.bfloat16)
    zero = jnp.zeros_like(weight)
    total = jnp.dot(
        jnp.where(near, weight, zero), values[:tokens], preferred_element_type=jnp.float32
    ) + jnp.dot(
        jnp.where(near, zero, weight), values[span * tokens :], preferred_element_type=jnp.float32
    )
    for d in range(1, span):
        weight = jnp.exp2(scores[d] * factor - peak).astype(jnp.bfloat16)
        total = total + jnp.dot(
            weight, values[d * tokens : (d + 1) * tokens], preferred_element_type=jnp.float32
        )
    out_ref[...] = (total[:, :HD] / total[:, HD:]).astype(jnp.bfloat16)


def attention(position, queries, pairs, span):
    tokens, width = queries.shape
    kv_here = pairs.shape[2] // (2 * HD)
    grouping = width // HD // kv_here
    keys = tokens * (span + 1)

    def block(distance, offset):
        return pl.BlockSpec(
            (1, tokens, HD),
            lambda h, i, at: (jnp.maximum(at[0] - distance, 0), 0, offset + h),
        )

    specs = [pl.BlockSpec((tokens, HD), lambda h, i, at: (0, h * grouping + i))]
    specs += [block(d, 0) for d in range(span + 1)]
    specs += [block(d, kv_here) for d in range(span + 1)]
    return pl.pallas_call(
        functools.partial(attention_kernel, span),
        grid_spec=pltpu.PrefetchScalarGridSpec(
            num_scalar_prefetch=1,
            grid=(kv_here, grouping),
            in_specs=specs,
            out_specs=pl.BlockSpec((tokens, HD), lambda h, i, at: (0, h * grouping + i)),
            scratch_shapes=[
                pltpu.VMEM((keys, 2 * HD), jnp.bfloat16),
                pltpu.VMEM((keys, 2 * HD), jnp.bfloat16),
                pltpu.VMEM((span, tokens, tokens), jnp.float32),
            ],
        ),
        out_shape=jax.ShapeDtypeStruct((tokens, width), jnp.bfloat16),
        compiler_params=params(),
        cost_estimate=pl.CostEstimate(
            flops=8 * width * tokens * keys,
            bytes_accessed=4 * tokens * width + 4 * keys * HD * kv_here,
            transcendentals=width // HD * tokens * keys,
        ),
        name="window_attention",
    )(position, queries, *([pairs] * (2 * span + 2)))


def per_device(
    conv_in,
    gate_in,
    q_proj,
    k_proj,
    v_proj,
    conv_weight,
    conv_bias,
    proj_dt_weight,
    proj_bc_weight,
    dt_gain,
    dt_weight,
    dt_bias,
    decay_rate,
    skip_weight,
):
    tokens, channels = conv_in.shape
    span = WINDOW // tokens
    rank = dt_gain.shape[0]
    state_count = decay_rate.shape[0]
    blocks = channels // GROUP

    tail = shifted(conv_in[tokens - (KCONV - 1) :], "seq", 1)
    tail = jnp.pad(tail, ((TAIL - (KCONV - 1), 0), (0, 0)))
    pairs = lax.all_gather(jnp.concatenate([k_proj, v_proj], axis=1), "seq")
    position = lax.axis_index("seq").astype(jnp.int32).reshape(1)

    act, sums = project(
        tail, conv_in, conv_weight, conv_bias[None], proj_dt_weight, proj_bc_weight
    )
    if lax.axis_size("tp") == 2:
        sums = sums + lax.ppermute(sums, "tp", [(0, 1), (1, 0)])
    else:
        sums = lax.psum(sums, "tp")
    bc = sums[:, rank : rank + 2 * state_count].reshape(-1)
    rates = (
        (decay_rate * -LOG2E).reshape(state_count, blocks, SUBLANES, LANES).transpose(1, 0, 2, 3)
    )
    y, cum, packed = local_scan(bc, sums, dt_gain[None], dt_weight, dt_bias[None], act, rates)
    everything = lax.all_gather(packed, "seq")
    attn_at, _ = lax.optimization_barrier((position, packed))
    attn_out = attention(attn_at, q_proj, pairs, span)
    finish_at, attn_out = lax.optimization_barrier((position, attn_out))
    mamba_out = finish(
        finish_at, bc, y, cum, rates, everything, act, gate_in, skip_weight[None]
    )
    return (mamba_out, attn_out)


def solution(mesh):
    return jax.shard_map(
        per_device,
        mesh=mesh,
        in_specs=(
            P("seq", "tp"),
            P("seq", "tp"),
            P("seq", "tp"),
            P("seq", "tp"),
            P("seq", "tp"),
            P(None, "tp"),
            P("tp"),
            P("tp", None),
            P(None, "tp"),
            P(),
            P(None, "tp"),
            P("tp"),
            P(None, "tp"),
            P("tp"),
        ),
        out_specs=(P("seq", "tp"), P("seq", "tp")),
        check_vma=False,
    )
```

time: 306 us -> 259 us (0.85)
  starting transfers between devices: 65.5 us -> 3.48 us
  between operations: 1.05 us -> 14.1 us
  Pallas kernels: 173 us -> 183 us
  waiting for transfers between devices: 54.4 us -> 50.3 us
    ppermute x18 -> x1, starting transfers between devices: 65.5 us -> 3.4 us  [shifted(): lax.ppermute(value, axis, [(source, source + steps) for source in range(c...]
    ppermute x18 -> x1, waiting for transfers between devices: 54.4 us -> 2.75 us  [shifted(): lax.ppermute(value, axis, [(source, source + steps) for source in range(c...]
    all_gather x0 -> x2, waiting for transfers between devices: none -> 46.3 us  [the longest x1 24.1 us: per_device(): pairs = lax.all_gather(jnp.concatenate([k_proj, v_proj], axis=1), 'seq')]
    pallas_call x1, Pallas kernels: 57.4 us -> 64 us  [local_scan(): pl.pallas_call(functools.partial(scan_kernel, rank, state_count), grid=(b...]
    pallas_call x4 -> x1, Pallas kernels: 61.9 us -> 64.6 us  [attention(): pl.pallas_call(functools.partial(attention_kernel, span), grid_spec=pltpu...]
  transfers between devices with their start and end apart: 19 -> 4, of which waited for: 5 -> 4; matrix products, arithmetic and copies ran while one was open for 2% -> 2% of each run, Pallas kernels for 40% -> 56%
where the time goes in v1:
time: 259 us; the launch traced here: 258 us
  Pallas kernels  183 us (71%)
  waiting for transfers between devices  50.3 us (19%)
  between operations  14.1 us (5%)
  local copies, waits for them, and re-layouts  3.51 us (1%)
  starting transfers between devices  3.48 us (1%)
  other arithmetic  3.08 us (1%)
    pallas_call x1, Pallas kernels, attention(): pl.pallas_call(functools.partial(attention_kernel, span), grid_spec=pltpu...  64.6 us
    pallas_call x1, Pallas kernels, local_scan(): pl.pallas_call(functools.partial(scan_kernel, rank, state_count), grid=(b...  64 us
    pallas_call x1, Pallas kernels, finish(): pl.pallas_call(functools.partial(finish_kernel, state_count), grid=(block...  39.8 us
    all_gather x1, waiting for transfers between devices, per_device(): pairs = lax.all_gather(jnp.concatenate([k_proj, v_proj], axis=1), 'seq')  24.1 us
    all_gather x1, waiting for transfers between devices, per_device(): everything = lax.all_gather(packed, 'seq')  22.2 us
    pallas_call x1, Pallas kernels, project(): pl.pallas_call(functools.partial(project_kernel, rank), grid=(blocks,), i...  14.7 us
  transfers between devices with their start and end apart: 4, of which 4 were waited for; matrix products, arithmetic and copies ran while one was open for 2% of the time, Pallas kernels for 56%

profile of v1, /device:TPU:18, one launch (start us, length us, event | category | flops | bytes accessed | tf_op | source)
XLA Modules:
  0.0 257.5 jit_solution(9587232602555962788)
XLA Ops:
  7.2 0.0 all-gather.5.cloned.1.call-start
  7.2 1.9 pad_maximum_fusion
  9.1 0.0 all-gather.5.cloned.1.call-update
  9.1 0.0 all-gather.7.cloned.1.call-start
  9.2 0.9 slice.6
  10.1 3.4 %collective-permute-start = (bf16[3,8192]{1,0:T(4,128)(2,1)S(1)}, bf16[3,8192]{1,0:T(4,128)(2,1)S(1)}, u32[]{:S(2)}, u32[]{:S(2)}) collective-permute-start(bf16[3,8192]{1,0:T(4,128)(2,1)S(1)} %slice.6), channel_id=1, source_target_pairs={{0,2},{2,4},{4,6},{6,8},{8,10},{10,12},{12,14},{14,16},{16,18},{18... | collective-permute-start | bytes 147464 | tf_op jit(solution)/shard_map/ppermute | solution.py:25
  13.5 2.8 %collective-permute-done = bf16[3,8192]{1,0:T(4,128)(2,1)S(1)} collective-permute-done((bf16[3,8192]{1,0:T(4,128)(2,1)S(1)}, bf16[3,8192]{1,0:T(4,128)(2,1)S(1)}, u32[]{:S(2)}, u32[]{:S(2)}) %collective-permute-start) | collective-permute-done | bytes 49184 | tf_op jit(solution)/shard_map/ppermute | solution.py:25
  16.3 0.8 pad.4.tail_ref
  17.0 14.7 %conv_and_projections.1 = (bf16[256,8192]{1,0:T(8,128)(2,1)}, f32[256,640]{1,0:T(8,128)}) custom-call(bf16[16,8192]{1,0:T(8,128)(2,1)} %pad.4.tail_ref, bf16[256,8192]{1,0:T(8,128)(2,1)} %x_ref.1, f32[4,8192]{1,0:T(4,128)} %taps_ref.1, f32[1,8192]{1,0:T(1,128)} %bitcast.35, bf16[8192,512]{1,0:T(8,128)(2,1)} %wdt_ref.2, bf16[32,8192]{1,0:T(8,128)(2,1)} %wbc_ref.1), custom_call_target="tpu_custom_call" | custom-call | flops 2281701376 | bytes 16777216 | tf_op jit(solution)/shard_map/conv_and_projections/pallas_call | solution.py:60
  31.7 0.0 collective-permute-start.1
  31.7 0.0 copy-done.1
  31.8 0.1 copy.18
  31.9 0.9 copy.20
  32.8 1.3 collective-permute-done.1
  34.0 1.2 add.5.low_ref
  35.2 0.0 copy-start
  35.2 0.8 reshape.14.bc_ref
  36.0 0.0 copy-done
  36.0 64.0 %local_scan.1 = (f32[8,2048,128]{2,1,0:T(8,128)}, f32[8,2048,128]{2,1,0:T(8,128)}, bf16[8,160,128]{2,1,0:T(8,128)(2,1)}) custom-call(f32[8192]{0:T(1024)} %reshape.14.bc_ref, f32[256,640]{1,0:T(8,128)} %copy-done, f32[1,512]{1,0:T(1,128)} %bitcast.39, bf16[512,8192]{1,0:T(8,128)(2,1)} %wdt_ref.3, f32[1,8192]{1,0:T(1,128)} %bitcast.37, ...), custom_call_target="tpu_custom_call" | custom-call | flops 2415919104 | bytes 33554432 | tf_op jit(solution)/shard_map/local_scan/pallas_call | solution.py:161
  100.0 0.0 all-gather.7.cloned.1.call-update
  100.0 24.1 %all-gather.5.cloned.1.call-done = bf16[4096,1024]{1,0:T(8,128)(2,1)} async-done(((bf16[256,1024]{1,0:T(8,128)(2,1)}), bf16[4096,1024]{1,0:T(8,128)(2,1)}) %all-gather.5.cloned.1.call-update) | async-done | bytes 8388624 | tf_op jit(solution)/shard_map/all_gather | solution.py:413
  124.2 64.6 %window_attention.1 = bf16[256,4096]{1,0:T(8,128)(2,1)} custom-call(s32[1]{0:T(128)} %bitcast.position, bf16[256,4096]{1,0:T(8,128)(2,1)} %q_ref.1, bf16[16,256,1024]{2,1,0:T(8,128)(2,1)} %bitcast.14, bf16[16,256,1024]{2,1,0:T(8,128)(2,1)} %bitcast.15, bf16[16,256,1024]{2,1,0:T(8,128)(2,1)} %bitcast.16, bf16[16,256,1024]{2,1,0:T(8,128)(2,1)} %bitcast.17, ...), custom_call_target="tpu_custom_call" | custom-call | flops 19327352832 | bytes 8912896 | tf_op jit(solution)/shard_map/window_attention/pallas_call | solution.py:365
  188.7 22.2 %all-gather.7.cloned.1.call-done = bf16[128,160,128]{2,1,0:T(8,128)(2,1)} async-done(((bf16[8,160,128]{2,1,0:T(8,128)(2,1)}), bf16[128,160,128]{2,1,0:T(8,128)(2,1)}) %all-gather.7.cloned.1.call-update) | async-done | bytes 5242896 | tf_op jit(solution)/shard_map/all_gather | solution.py:428
  210.9 39.8 %carry_and_gate.1 = bf16[256,8192]{1,0:T(8,128)(2,1)} custom-call(s32[1]{0:T(128)} %bitcast.position, f32[8192]{0:T(1024)} %reshape.14.bc_ref, f32[8,2048,128]{2,1,0:T(8,128)} %get-tuple-element.15.y_ref, f32[8,2048,128]{2,1,0:T(8,128)} %get-tuple-element.16.cum_ref, f32[8,16,8,128]{3,2,1,0:T(8,128)} %bitcast.34, bf16[16,8,160,128]{3,2,1,0:T(8,128)(2,1)} %bitcast.36, ...), custom_call_target="tpu_custom_call" | custom-call | flops 201326592 | bytes 29360128 | tf_op jit(solution)/shard_map/carry_and_gate/pallas_call | solution.py:265
  (3 shorter events, 0.1 us)
Async XLA Ops:
  7.2 117.0 %all-gather.5.cloned.1.call-start = ((), (), s32[]{:S(2)}) async-start(), calls=%async_computation | async-start | bytes 8912896 | tf_op jit(solution)/shard_map/all_gather | solution.py:413
  9.1 201.8 %all-gather.7.cloned.1.call-start = ((), (), s32[]{:S(2)}) async-start(), calls=%async_computation.1 | async-start | bytes 5570560 | tf_op jit(solution)/shard_map/all_gather | solution.py:428
  10.1 6.2 %collective-permute-start = (bf16[3,8192]{1,0:T(4,128)(2,1)S(1)}, bf16[3,8192]{1,0:T(4,128)(2,1)S(1)}, u32[]{:S(2)}, u32[]{:S(2)}) collective-permute-start(bf16[3,8192]{1,0:T(4,128)(2,1)S(1)} %slice.6), channel_id=1, source_target_pairs={{0,2},{2,4},{4,6},{6,8},{8,10},{10,12},{12,14},{14,16},{16,18},{18... | collective-permute-start | bytes 147464 | tf_op jit(solution)/shard_map/ppermute | solution.py:25
  17.0 14.7 %copy-start.1 = (f32[16,8192]{1,0:T(8,128)S(1)}, f32[16,8192]{1,0:T(8,128)}, u32[]{:S(2)}) copy-start(f32[16,8192]{1,0:T(8,128)} %param.26) | copy-start | bytes 1572868
  31.7 2.3 collective-permute-start.1
  35.2 0.8 copy-start
Sparse Core Ops, SparseCore 0:
  11.3 112.7 all-gather.4
  126.9 83.9 all-gather.6

commit v2 on v1

--- a/solution.py
+++ b/solution.py
@@ -131,7 +131,7 @@
 
     zero = jnp.zeros((SUBLANES, LANES), jnp.float32)
     through, hidden = lax.fori_loop(
-        0, tokens, advance, ((zero,) * pair, (zero,) * (state_count * pair)), unroll=2
+        0, tokens, advance, ((zero,) * pair, (zero,) * (state_count * pair)), unroll=4
     )
     size = 2 * SUBLANES
     for p in range(pair):
@@ -155,7 +155,7 @@
     rank = gain.shape[1]
     blocks, state_count = rates.shape[:2]
     rows = tokens * SUBLANES
-    pair = 2 if blocks % 2 == 0 else 1
+    pair = 1
     width = pair * GROUP
     packed = (state_count + 4) * SUBLANES
     return pl.pallas_call(
@@ -195,10 +195,54 @@
     )(bc, low, gain, wdt, bias, act, rates)
 
 
+def join_kernel(state_count, rate_ref, first_ref, second_ref, out_ref):
+    size = 2 * SUBLANES
+    mark = state_count // 2 * size
+
+    def elapsed(ref):
+        parts = ref[0, mark : mark + 2 * size].astype(jnp.float32)
+        return parts[:SUBLANES] + parts[SUBLANES:size] + parts[size : size + SUBLANES]
+
+    later = elapsed(second_ref)
+    total = elapsed(first_ref) + later
+    for n in range(0, state_count, 2):
+        rows = slice(n // 2 * size, (n // 2 + 1) * size)
+        rate = jnp.concatenate([rate_ref[0, n], rate_ref[0, n + 1]], axis=0)
+        both = jnp.concatenate([later, later], axis=0)
+        joined = jnp.exp2(rate * both) * first_ref[0, rows].astype(jnp.float32)
+        out_ref[0, rows] = (joined + second_ref[0, rows].astype(jnp.float32)).astype(jnp.bfloat16)
+    high = total.astype(jnp.bfloat16).astype(jnp.float32)
+    middle = (total - high).astype(jnp.bfloat16).astype(jnp.float32)
+    low = total - high - middle
+    out_ref[0, mark : mark + size] = jnp.concatenate([high, middle], axis=0).astype(jnp.bfloat16)
+    out_ref[0, mark + size : mark + 2 * size] = jnp.concatenate(
+        [low, jnp.zeros_like(low)], axis=0
+    ).astype(jnp.bfloat16)
+
+
+def join(rates, first, second):
+    blocks, packed, _ = first.shape
+    state_count = rates.shape[1]
+    part = pl.BlockSpec((1, packed, LANES), lambda i: (i, 0, 0))
+    return pl.pallas_call(
+        functools.partial(join_kernel, state_count),
+        grid=(blocks,),
+        in_specs=[
+            pl.BlockSpec((1, state_count, SUBLANES, LANES), lambda i: (i, 0, 0, 0)),
+            part,
+            part,
+        ],
+        out_specs=part,
+        out_shape=jax.ShapeDtypeStruct(first.shape, jnp.bfloat16),
+        compiler_params=params(),
+        name="join_states",
+    )(rates, first, second)
+
+
 TOKENS_AT_ONCE = 4
 
 
-def finish_kernel(state_count, position, bc_ref, y_ref, cum_ref, rate_ref, all_ref, act_ref, gate_ref,
+def finish_kernel(state_count, count, bc_ref, y_ref, cum_ref, rate_ref, all_ref, act_ref, gate_ref,
                   skip_ref, out_ref, mixed, enter):
     tokens = act_ref.shape[0]
     pair = rate_ref.shape[0]
@@ -222,7 +266,7 @@
             return tuple(new)
 
         zero = jnp.zeros((SUBLANES, LANES), jnp.float32)
-        held = lax.fori_loop(0, position[0], compose, (zero,) * state_count)
+        held = lax.fori_loop(0, count[0], compose, (zero,) * state_count)
         for n in range(state_count):
             enter[p, n] = held[n]
 
@@ -255,7 +299,7 @@
         out_ref[:, cols] = (value * (gate / (1.0 + jnp.exp(-gate)))).astype(jnp.bfloat16)
 
 
-def finish(position, bc, y, cum, rates, everything, act, gate, skip):
+def finish(count, bc, y, cum, rates, everything, act, gate, skip):
     tokens, channels = act.shape
     blocks, state_count = rates.shape[:2]
     rows = tokens * SUBLANES
@@ -289,7 +333,7 @@
             transcendentals=tokens * channels * state_count,
         ),
         name="carry_and_gate",
-    )(position, bc, y, cum, rates, everything, act, gate, skip)
+    )(count, bc, y, cum, rates, everything, act, gate, skip)
 
 
 def attention_kernel(span, position, q_ref, *refs):
@@ -425,10 +469,14 @@
         (decay_rate * -LOG2E).reshape(state_count, blocks, SUBLANES, LANES).transpose(1, 0, 2, 3)
     )
     y, cum, packed = local_scan(bc, sums, dt_gain[None], dt_weight, dt_bias[None], act, rates)
-    everything = lax.all_gather(packed, "seq")
-    attn_at, _ = lax.optimization_barrier((position, packed))
+    joined = join(rates, shifted(packed, "seq", 2), shifted(packed, "seq", 1))
+    seq = lax.axis_size("seq")
+    everything = lax.all_gather(
+        joined, "seq", axis_index_groups=[list(range(0, seq, 2)), list(range(1, seq, 2))]
+    )
+    attn_at, _ = lax.optimization_barrier((position, joined))
     attn_out = attention(attn_at, q_proj, pairs, span)
-    finish_at, attn_out = lax.optimization_barrier((position, attn_out))
+    finish_at, attn_out = lax.optimization_barrier((position // 2 + 1, attn_out))
     mamba_out = finish(
         finish_at, bc, y, cum, rates, everything, act, gate_in, skip_weight[None]
     )

time: 259 us -> 254 us (0.981)
  waiting for transfers between devices: 50.3 us -> 39 us
  starting transfers between devices: 3.48 us -> 12 us
  Pallas kernels: 183 us -> 180 us
    ppermute x1 -> x3, waiting for transfers between devices: 2.75 us -> 37.7 us  [shifted(): lax.ppermute(value, axis, [(source, source + steps) for source in range(c...]
    all_gather x1, waiting for transfers between devices: 24.1 us -> 0.02 us  [per_device(): pairs = lax.all_gather(jnp.concatenate([k_proj, v_proj], axis=1), 'seq')]
    all_gather x1, waiting for transfers between devices: 22.2 us -> 0.02 us  [per_device(): lax.all_gather(joined, 'seq', axis_index_groups=[list(range(0, seq, 2)),...]
    ppermute x1 -> x3, starting transfers between devices: 3.4 us -> 12 us  [shifted(): lax.ppermute(value, axis, [(source, source + steps) for source in range(c...]
    pallas_call x1, Pallas kernels: 64 us -> 57.3 us  [local_scan(): pl.pallas_call(functools.partial(scan_kernel, rank, state_count), grid=(b...]
    pallas_call x0 -> x1, Pallas kernels: none -> 4.88 us  [join(): pl.pallas_call(functools.partial(join_kernel, state_count), grid=(blocks,...]
  transfers between devices with their start and end apart: 4 -> 6, of which waited for: 4 -> 4; matrix products, arithmetic and copies ran while one was open for 2% -> 2% of each run, Pallas kernels for 56% -> 56%
where the time goes in v2:
time: 254 us; the launch traced here: 253 us
  Pallas kernels  180 us (71%)
  waiting for transfers between devices  39 us (15%)
  between operations  14.2 us (6%)
  starting transfers between devices  12 us (5%)
  local copies, waits for them, and re-layouts  4.2 us (2%)
  other arithmetic  3.08 us (1%)
    pallas_call x1, Pallas kernels, attention(): pl.pallas_call(functools.partial(attention_kernel, span), grid_spec=pltpu...  64.6 us
    pallas_call x1, Pallas kernels, local_scan(): pl.pallas_call(functools.partial(scan_kernel, rank, state_count), grid=(b...  57.3 us
    pallas_call x1, Pallas kernels, finish(): pl.pallas_call(functools.partial(finish_kernel, state_count), grid=(block...  38.9 us
    ppermute x3, waiting for transfers between devices, shifted(): lax.ppermute(value, axis, [(source, source + steps) for source in range(c...  37.7 us
    pallas_call x1, Pallas kernels, project(): pl.pallas_call(functools.partial(project_kernel, rank), grid=(blocks,), i...  14.7 us
    ppermute x3, starting transfers between devices, shifted(): lax.ppermute(value, axis, [(source, source + steps) for source in range(c...  12 us
  transfers between devices with their start and end apart: 6, of which 4 were waited for; matrix products, arithmetic and copies ran while one was open for 2% of the time, Pallas kernels for 56%

profile of v2, /device:TPU:18, one launch (start us, length us, event | category | flops | bytes accessed | tf_op | source)
XLA Modules:
  0.0 252.9 jit_solution(3581993193660062815)
XLA Ops:
  7.2 0.0 all-gather.5.cloned.1.call-start
  7.2 1.9 pad_maximum_fusion
  9.1 0.0 all-gather.7.cloned.1.call-start
  9.2 0.9 slice.6
  10.1 3.4 %collective-permute-start = (bf16[3,8192]{1,0:T(4,128)(2,1)S(1)}, bf16[3,8192]{1,0:T(4,128)(2,1)S(1)}, u32[]{:S(2)}, u32[]{:S(2)}) collective-permute-start(bf16[3,8192]{1,0:T(4,128)(2,1)S(1)} %slice.6), channel_id=1, source_target_pairs={{0,2},{2,4},{4,6},{6,8},{8,10},{10,12},{12,14},{14,16},{16,18},{18... | collective-permute-start | bytes 147464 | tf_op jit(solution)/shard_map/ppermute | solution.py:25
  13.5 2.8 %collective-permute-done = bf16[3,8192]{1,0:T(4,128)(2,1)S(1)} collective-permute-done((bf16[3,8192]{1,0:T(4,128)(2,1)S(1)}, bf16[3,8192]{1,0:T(4,128)(2,1)S(1)}, u32[]{:S(2)}, u32[]{:S(2)}) %collective-permute-start) | collective-permute-done | bytes 49184 | tf_op jit(solution)/shard_map/ppermute | solution.py:25
  16.3 0.7 pad.4.tail_ref
  17.0 14.7 %conv_and_projections.1 = (bf16[256,8192]{1,0:T(8,128)(2,1)}, f32[256,640]{1,0:T(8,128)}) custom-call(bf16[16,8192]{1,0:T(8,128)(2,1)} %pad.4.tail_ref, bf16[256,8192]{1,0:T(8,128)(2,1)} %x_ref.1, f32[4,8192]{1,0:T(4,128)} %taps_ref.1, f32[1,8192]{1,0:T(1,128)} %bitcast.36, bf16[8192,512]{1,0:T(8,128)(2,1)} %wdt_ref.2, bf16[32,8192]{1,0:T(8,128)(2,1)} %wbc_ref.1), custom_call_target="tpu_custom_call" | custom-call | flops 2281701376 | bytes 16777216 | tf_op jit(solution)/shard_map/conv_and_projections/pallas_call | solution.py:60
  31.8 0.1 copy.18
  31.9 0.9 copy.20
  32.7 1.3 collective-permute-done.1
  34.0 1.2 add.10.low_ref
  35.2 0.8 reshape.19.bc_ref
  36.0 0.0 copy-done
  36.0 57.3 %local_scan.1 = (f32[8,2048,128]{2,1,0:T(8,128)}, f32[8,2048,128]{2,1,0:T(8,128)}, bf16[8,160,128]{2,1,0:T(8,128)(2,1)}) custom-call(f32[8192]{0:T(1024)} %reshape.19.bc_ref, f32[256,640]{1,0:T(8,128)} %copy-done, f32[1,512]{1,0:T(1,128)} %bitcast.40, bf16[512,8192]{1,0:T(8,128)(2,1)} %wdt_ref.3, f32[1,8192]{1,0:T(1,128)} %bitcast.38, ...), custom_call_target="tpu_custom_call" | custom-call | flops 2415919104 | bytes 33554432 | tf_op jit(solution)/shard_map/local_scan/pallas_call | solution.py:161
  93.3 4.2 %collective-permute-start.3 = (bf16[8,160,128]{2,1,0:T(8,128)(2,1)}, bf16[8,160,128]{2,1,0:T(8,128)(2,1)S(1)}, u32[]{:S(2)}, u32[]{:S(2)}) collective-permute-start(bf16[8,160,128]{2,1,0:T(8,128)(2,1)} %get-tuple-element.12), channel_id=1, source_target_pairs={{0,2},{2,4},{4,6},{6,8},{8,10},{10,12},{12,14},{14,16},{16,18},{18... | collective-permute-start | bytes 983048 | tf_op jit(solution)/shard_map/ppermute | solution.py:25
  97.5 4.4 %collective-permute-start.2 = (bf16[8,160,128]{2,1,0:T(8,128)(2,1)}, bf16[8,160,128]{2,1,0:T(8,128)(2,1)S(1)}, u32[]{:S(2)}, u32[]{:S(2)}) collective-permute-start(bf16[8,160,128]{2,1,0:T(8,128)(2,1)} %get-tuple-element.12), channel_id=1, source_target_pairs={{0,4},{2,6},{4,8},{6,10},{8,12},{10,14},{12,16},{14,18},{16,20},{1... | collective-permute-start | bytes 983048 | tf_op jit(solution)/shard_map/ppermute | solution.py:25
  101.9 10.2 %collective-permute-done.3.second_ref = bf16[8,160,128]{2,1,0:T(8,128)(2,1)S(1)} collective-permute-done((bf16[8,160,128]{2,1,0:T(8,128)(2,1)}, bf16[8,160,128]{2,1,0:T(8,128)(2,1)S(1)}, u32[]{:S(2)}, u32[]{:S(2)}) %collective-permute-start.3) | collective-permute-done | bytes 327712 | tf_op jit(solution)/shard_map/ppermute | solution.py:25
  112.1 24.8 %collective-permute-done.2.first_ref = bf16[8,160,128]{2,1,0:T(8,128)(2,1)S(1)} collective-permute-done((bf16[8,160,128]{2,1,0:T(8,128)(2,1)}, bf16[8,160,128]{2,1,0:T(8,128)(2,1)S(1)}, u32[]{:S(2)}, u32[]{:S(2)}) %collective-permute-start.2) | collective-permute-done | bytes 327712 | tf_op jit(solution)/shard_map/ppermute | solution.py:25
  136.8 0.7 copy-done.3
  137.6 4.9 %join_states.1 = bf16[8,160,128]{2,1,0:T(8,128)(2,1)} custom-call(f32[8,16,8,128]{3,2,1,0:T(8,128)} %bitcast.33, bf16[8,160,128]{2,1,0:T(8,128)(2,1)} %copy-done.3, bf16[8,160,128]{2,1,0:T(8,128)(2,1)} %copy-done.2), custom_call_target="tpu_custom_call" | custom-call | tf_op jit(solution)/shard_map/join_states/pallas_call | solution.py:227
  142.5 0.0 all-gather.5.cloned.1.call-done
  142.5 64.6 %window_attention.1 = bf16[256,4096]{1,0:T(8,128)(2,1)} custom-call(s32[1]{0:T(128)} %bitcast.position, bf16[256,4096]{1,0:T(8,128)(2,1)} %q_ref.1, bf16[16,256,1024]{2,1,0:T(8,128)(2,1)} %bitcast.14, bf16[16,256,1024]{2,1,0:T(8,128)(2,1)} %bitcast.15, bf16[16,256,1024]{2,1,0:T(8,128)(2,1)} %bitcast.16, bf16[16,256,1024]{2,1,0:T(8,128)(2,1)} %bitcast.17, ...), custom_call_target="tpu_custom_call" | custom-call | flops 19327352832 | bytes 8912896 | tf_op jit(solution)/shard_map/window_attention/pallas_call | solution.py:409
  207.1 38.9 %carry_and_gate.1 = bf16[256,8192]{1,0:T(8,128)(2,1)} custom-call(s32[1]{0:T(128)S(6)} %add.9.count, f32[8192]{0:T(1024)} %reshape.19.bc_ref, f32[8,2048,128]{2,1,0:T(8,128)} %get-tuple-element.15.y_ref, f32[8,2048,128]{2,1,0:T(8,128)} %get-tuple-element.16.cum_ref, f32[8,16,8,128]{3,2,1,0:T(8,128)} %bitcast.34, bf16[8,8,160,128]{3,2,1,0:T(8,128)(2,1)} %bitcast.37, ...), custom_call_target="tpu_custom_call" | custom-call | flops 201326592 | bytes 29360128 | tf_op jit(solution)/shard_map/carry_and_gate/pallas_call | solution.py:309
  (12 shorter events, 0.1 us)
Async XLA Ops:
  7.2 135.4 %all-gather.5.cloned.1.call-start = ((), (), s32[]{:S(2)}) async-start(), calls=%async_computation | async-start | bytes 8912896 | tf_op jit(solution)/shard_map/all_gather | solution.py:457
  9.1 198.0 %all-gather.7.cloned.1.call-start = ((), (), s32[]{:S(2)}) async-start(), calls=%async_computation.1 | async-start | bytes 2949120 | tf_op jit(solution)/shard_map/all_gather | solution.py:474
  10.1 6.2 %collective-permute-start = (bf16[3,8192]{1,0:T(4,128)(2,1)S(1)}, bf16[3,8192]{1,0:T(4,128)(2,1)S(1)}, u32[]{:S(2)}, u32[]{:S(2)}) collective-permute-start(bf16[3,8192]{1,0:T(4,128)(2,1)S(1)} %slice.6), channel_id=1, source_target_pairs={{0,2},{2,4},{4,6},{6,8},{8,10},{10,12},{12,14},{14,16},{16,18},{18... | collective-permute-start | bytes 147464 | tf_op jit(solution)/shard_map/ppermute | solution.py:25
  17.0 14.7 %copy-start.1 = (f32[16,8192]{1,0:T(8,128)S(1)}, f32[16,8192]{1,0:T(8,128)}, u32[]{:S(2)}) copy-start(f32[16,8192]{1,0:T(8,128)} %param.26) | copy-start | bytes 1572868
  31.7 2.3 collective-permute-start.1
  35.2 0.8 copy-start
  93.3 18.7 %collective-permute-start.3 = (bf16[8,160,128]{2,1,0:T(8,128)(2,1)}, bf16[8,160,128]{2,1,0:T(8,128)(2,1)S(1)}, u32[]{:S(2)}, u32[]{:S(2)}) collective-permute-start(bf16[8,160,128]{2,1,0:T(8,128)(2,1)} %get-tuple-element.12), channel_id=1, source_target_pairs={{0,2},{2,4},{4,6},{6,8},{8,10},{10,12},{12,14},{14,16},{16,18},{18... | collective-permute-start | bytes 983048 | tf_op jit(solution)/shard_map/ppermute | solution.py:25
  97.5 39.3 %collective-permute-start.2 = (bf16[8,160,128]{2,1,0:T(8,128)(2,1)}, bf16[8,160,128]{2,1,0:T(8,128)(2,1)S(1)}, u32[]{:S(2)}, u32[]{:S(2)}) collective-permute-start(bf16[8,160,128]{2,1,0:T(8,128)(2,1)} %get-tuple-element.12), channel_id=1, source_target_pairs={{0,4},{2,6},{4,8},{6,10},{8,12},{10,14},{12,16},{14,18},{16,20},{1... | collective-permute-start | bytes 983048 | tf_op jit(solution)/shard_map/ppermute | solution.py:25
  112.1 24.8 %copy-start.2 = (bf16[8,160,128]{2,1,0:T(8,128)(2,1)}, bf16[8,160,128]{2,1,0:T(8,128)(2,1)S(1)}, u32[]{:S(2)}) copy-start(bf16[8,160,128]{2,1,0:T(8,128)(2,1)S(1)} %collective-permute-done.3.second_ref) | copy-start | bytes 983044
  136.8 0.7 copy-start.3
Sparse Core Ops, SparseCore 0:
  11.3 117.8 all-gather.4
  142.6 53.2 all-gather.6
